TPU v7x, 512 devices: a whole 4x4x16 slice. The times are simulated.
512 devices in a mesh: head: 8 (over x, core), tok: 64 (over z, y).
Axes of the slice: x: 4, y: 4, z: 16, core: 2. Of those that a mesh axis runs over, the one named last changes fastest.
Arguments:
- query_one: bfloat16 [16384, 4096], P(('head', 'tok')), may hold values from -6 to 6
- key_one: bfloat16 [16384, 4096], P(('head', 'tok')), may hold values from -6 to 6
- value_one: bfloat16 [16384, 4096], P(('head', 'tok')), may hold values from -6 to 6
- rate_one: bfloat16 [16384, 8], P(('head', 'tok')), may hold values from 0.099609375 to 1
- query_two: bfloat16 [16384, 4096], P(('head', 'tok')), may hold values from -6 to 6
- w_gate: float32 [8, 512, 512], P('head', 'tok'), may hold values from -0.25 to 0.25
- w_up: float32 [8, 512, 512], P('head', 'tok'), may hold values from -0.25 to 0.25
- w_down: float32 [8, 512, 512], P('head', 'tok'), may hold values from -0.25 to 0.25
- step_size: float32 [8], P('head'), may hold values from 0.02 to 0.08
Outputs:
- out_one: bfloat16 [16384, 4096], P(('head', 'tok'))
- out_two: bfloat16 [16384, 4096], P(('head', 'tok'))
- gate_new: float32 [8, 512, 512], P('head', 'tok')
- up_new: float32 [8, 512, 512], P('head', 'tok')
- down_new: float32 [8, 512, 512], P('head', 'tok')
All inputs are finite; a program needn't handle non-finite values.
Results may differ from a plain program's by a relative error of at most 0.011.
Values may be sent and summed in bfloat16 or wider, within the bound.
A program may use at most 64 MiB of HBM per device.

v0:
```python
import jax
import jax.numpy as jnp
from jax import lax
from jax.sharding import PartitionSpec as P


def apply_piece(query, gate_b, up_b, down_b):
    pre_gate = jnp.einsum("thd,hjd->htj", query, gate_b, preferred_element_type=jnp.float32)
    pre_up = jnp.einsum("thd,hjd->htj", query, up_b, preferred_element_type=jnp.float32)
    hidden = (pre_gate * jax.nn.sigmoid(pre_gate) * pre_up).astype(jnp.bfloat16)
    return jnp.einsum("htj,hjd->thd", hidden, down_b, preferred_element_type=jnp.float32)


def forward_piece(query, keys, targets, gate_b, up_b, down_b):
    out_term = apply_piece(query, gate_b, up_b, down_b)
    key_gate = jnp.einsum("thd,hjd->htj", keys, gate_b, preferred_element_type=jnp.float32)
    key_up = jnp.einsum("thd,hjd->htj", keys, up_b, preferred_element_type=jnp.float32)
    sigmoid_k = jax.nn.sigmoid(key_gate)
    act_k = key_gate * sigmoid_k
    hidden_k = (act_k * key_up).astype(jnp.bfloat16)
    back = jnp.einsum("thd,hjd->htj", targets, down_b, preferred_element_type=jnp.float32)
    grad_gate_pre = (back * key_up * sigmoid_k * (1.0 + key_gate * (1.0 - sigmoid_k))).astype(
        jnp.bfloat16
    )
    grad_up_pre = (back * act_k).astype(jnp.bfloat16)
    return (out_term, grad_gate_pre, grad_up_pre, hidden_k)


def gradient_rows(gate_all, up_all, hidden_all, keys, targets):
    grad_gate = jnp.einsum("htj,thd->jhd", gate_all, keys, preferred_element_type=jnp.float32)
    grad_up = jnp.einsum("htj,thd->jhd", up_all, keys, preferred_element_type=jnp.float32)
    grad_down = jnp.einsum("htj,thd->jhd", hidden_all, targets, preferred_element_type=jnp.float32)
    return jnp.stack([grad_gate, grad_up, grad_down], axis=2)


def renew(weights, grad_rows, step_size):
    grads = jnp.moveaxis(grad_rows, 0, 1)
    scale = jnp.sqrt(jnp.mean(grads * grads, axis=2, keepdims=True) + 1e-06)
    return weights - step_size[:, None, None] * grads / scale


def local(query_one, key_one, value_one, rate_one, query_two, w_gate, w_up, w_down, step_size):
    heads_local = w_gate.shape[0]
    width = w_gate.shape[2]
    moved = (
        lax.all_to_all(query_one, "head", split_axis=1, concat_axis=0, tiled=True),
        lax.all_to_all(key_one, "head", split_axis=1, concat_axis=0, tiled=True),
        lax.all_to_all(value_one, "head", split_axis=1, concat_axis=0, tiled=True),
        lax.all_to_all(rate_one, "head", split_axis=1, concat_axis=0, tiled=True),
        lax.all_to_all(query_two, "head", split_axis=1, concat_axis=0, tiled=True),
    )
    tokens = moved[0].shape[0]
    query_a = moved[0].reshape(tokens, heads_local, width)
    keys = moved[1].reshape(tokens, heads_local, width)
    values = moved[2].reshape(tokens, heads_local, width)
    rates = moved[3].astype(jnp.float32)
    query_b = moved[4].reshape(tokens, heads_local, width)
    targets = (-(rates[:, :, None] * values.astype(jnp.float32))).astype(jnp.bfloat16)
    pieces = (
        lax.all_gather(w_gate.astype(jnp.bfloat16), "tok", axis=1, tiled=True),
        lax.all_gather(w_up.astype(jnp.bfloat16), "tok", axis=1, tiled=True),
        lax.all_gather(w_down.astype(jnp.bfloat16), "tok", axis=1, tiled=True),
    )
    out_term, grad_gate_pre, grad_up_pre, hidden_k = forward_piece(
        query_a, keys, targets, pieces[0], pieces[1], pieces[2]
    )
    first_block = out_term.reshape(tokens, heads_local * width).astype(jnp.bfloat16)
    grad_local = lax.psum_scatter(
        gradient_rows(grad_gate_pre, grad_up_pre, hidden_k, keys, targets),
        "tok",
        scatter_dimension=0,
        tiled=True,
    )
    gate_new = renew(w_gate, grad_local[:, :, 0, :], step_size)
    up_new = renew(w_up, grad_local[:, :, 1, :], step_size)
    down_new = renew(w_down, grad_local[:, :, 2, :], step_size)
    pieces = (
        lax.all_gather(gate_new.astype(jnp.bfloat16), "tok", axis=1, tiled=True),
        lax.all_gather(up_new.astype(jnp.bfloat16), "tok", axis=1, tiled=True),
        lax.all_gather(down_new.astype(jnp.bfloat16), "tok", axis=1, tiled=True),
    )
    second_total = apply_piece(query_b, pieces[0], pieces[1], pieces[2])
    second_block = second_total.reshape(tokens, heads_local * width).astype(jnp.bfloat16)
    first_back, second_back = (
        lax.all_to_all(first_block, "head", split_axis=0, concat_axis=1, tiled=True),
        lax.all_to_all(second_block, "head", split_axis=0, concat_axis=1, tiled=True),
    )
    return (first_back, second_back, gate_new, up_new, down_new)


def solution(mesh):
    in_specs = (
        P(("head", "tok"), None),
        P(("head", "tok"), None),
        P(("head", "tok"), None),
        P(("head", "tok"), None),
        P(("head", "tok"), None),
        P("head", "tok", None),
        P("head", "tok", None),
        P("head", "tok", None),
        P("head"),
    )
    out_specs = (
        P(("head", "tok"), None),
        P(("head", "tok"), None),
        P("head", "tok", None),
        P("head", "tok", None),
        P("head", "tok", None),
    )
    return jax.shard_map(local, mesh=mesh, in_specs=in_specs, out_specs=out_specs, check_vma=False)
```

profile of v0, /device:TPU:1, one launch (start us, length us, event | category | flops | bytes accessed | tf_op | source)
XLA Modules:
  0.0 1364.1 jit_solution(18135310961557693874)
XLA Ops:
  7.2 1.3 copy.43
  8.4 10.1 all-to-all-start.2
  18.5 0.7 convert_element_type.143
  19.3 76.5 %all_gather.20 = bf16[1,512,512]{2,1,0:T(8,128)(2,1)S(1)} all-gather(bf16[1,8,512]{2,1,0:T(8,128)(2,1)S(1)} %convert_element_type.143), channel_id=1, replica_groups=mesh['head'=8,'tok'=64] {'tok'}, dimensions={1}, use_global_device_ids=true | all-gather | bytes 532480 | tf_op jit(solution)/shard_map/all_gather | solution.py:62
  95.8 0.7 convert_element_type.141
  96.5 73.1 %all_gather.19 = bf16[1,512,512]{2,1,0:T(8,128)(2,1)S(1)} all-gather(bf16[1,8,512]{2,1,0:T(8,128)(2,1)S(1)} %convert_element_type.141), channel_id=1, replica_groups=mesh['head'=8,'tok'=64] {'tok'}, dimensions={1}, use_global_device_ids=true | all-gather | bytes 532480 | tf_op jit(solution)/shard_map/all_gather | solution.py:61
  169.7 0.7 convert_element_type.140
  170.4 1.7 copy.66
  172.0 1.7 copy.65
  173.7 0.0 all-to-all-done.2
  173.7 55.9 %all-to-all-start.4 = ((bf16[32,8,512]{2,0,1:T(8,128)(2,1)}), bf16[32,8,512]{2,0,1:T(8,128)(2,1)S(1)}, u32[]{:S(2)}, u32[]{:S(2)}) async-start(bf16[32,8,512]{2,0,1:T(8,128)(2,1)} %bitcast.139), calls=%async_computation.4 | async-start | bytes 524288 | tf_op jit(solution)/shard_map/all_to_all | solution.py:47
  229.7 71.9 %all_gather.18 = bf16[1,512,512]{2,1,0:T(8,128)(2,1)S(1)} all-gather(bf16[1,8,512]{2,1,0:T(8,128)(2,1)S(1)} %convert_element_type.140), channel_id=1, replica_groups=mesh['head'=8,'tok'=64] {'tok'}, dimensions={1}, use_global_device_ids=true | all-gather | bytes 532480 | tf_op jit(solution)/shard_map/all_gather | solution.py:60
  301.6 0.1 reshape.421
  301.7 0.0 all-to-all-done.4
  301.7 30.4 %all-to-all-start.3 = ((bf16[32,8,512]{2,0,1:T(8,128)(2,1)}), bf16[32,8,512]{2,0,1:T(8,128)(2,1)S(1)}, u32[]{:S(2)}, u32[]{:S(2)}) async-start(bf16[32,8,512]{2,0,1:T(8,128)(2,1)} %bitcast.140), calls=%async_computation.3 | async-start | bytes 524288 | tf_op jit(solution)/shard_map/all_to_all | solution.py:48
  332.0 0.3 fusion.12
  332.4 0.3 fusion.16
  332.7 5.8 all-to-all-done.3
  338.6 0.3 fusion.9
  338.9 0.4 convolution_bitcast_fusion.1
  339.3 0.4 convolution_bitcast_fusion.2
  339.8 0.1 fusion.4
  339.9 0.4 convolution_bitcast_fusion
  340.3 1.9 pad_maximum_fusion
  342.2 0.0 reduce-scatter.2.cloned.1.call-update
  342.2 0.9 copy-done
  343.2 0.7 copy.67
  343.9 4.4 all-to-all-start
  348.3 0.0 copy-start.4
  348.3 0.7 copy.64
  349.7 5.1 all-to-all-done
  354.8 4.4 all-to-all-start.5
  359.1 0.3 fusion.18
  359.5 1.3 convolution_convert_fusion.1
  360.7 665.9 %reduce-scatter.2.cloned.1.call-done = f32[8,1,3,512]{3,0,2,1:T(8,128)} async-done(((f32[512,1,3,512]{3,0,2,1:T(8,128)}), f32[8,1,3,512]{3,0,2,1:T(8,128)}) %reduce-scatter.2.cloned.1.call-update) | async-done | bytes 49168 | tf_op jit(solution)/shard_map/reduce_scatter | solution.py:68
  1026.6 0.9 multiply_reduce_fusion.1
  1027.6 1.5 fusion.47
  1029.0 72.6 %all_gather.23 = bf16[1,512,512]{2,1,0:T(8,128)(2,1)S(1)} all-gather(bf16[1,8,512]{2,1,0:T(8,128)(2,1)S(1)} %get-tuple-element.14), channel_id=1, replica_groups=mesh['head'=8,'tok'=64] {'tok'}, dimensions={1}, use_global_device_ids=true | all-gather | bytes 532480 | tf_op jit(solution)/shard_map/all_gather | solution.py:79
  1101.6 73.4 %all_gather.21 = bf16[1,512,512]{2,1,0:T(8,128)(2,1)S(1)} all-gather(bf16[1,8,512]{2,1,0:T(8,128)(2,1)S(1)} %get-tuple-element.16), channel_id=1, replica_groups=mesh['head'=8,'tok'=64] {'tok'}, dimensions={1}, use_global_device_ids=true | all-gather | bytes 532480 | tf_op jit(solution)/shard_map/all_gather | solution.py:80
  1175.0 72.8 %all_gather.22 = bf16[1,512,512]{2,1,0:T(8,128)(2,1)S(1)} all-gather(bf16[1,8,512]{2,1,0:T(8,128)(2,1)S(1)} %get-tuple-element.8), channel_id=1, replica_groups=mesh['head'=8,'tok'=64] {'tok'}, dimensions={1}, use_global_device_ids=true | all-gather | bytes 532480 | tf_op jit(solution)/shard_map/all_gather | solution.py:78
  1247.8 91.3 %all-to-all-start.1 = ((bf16[8,32,512]{2,1,0:T(8,128)(2,1)}), bf16[8,32,512]{2,1,0:T(8,128)(2,1)S(1)}, u32[]{:S(2)}, u32[]{:S(2)}) async-start(bf16[8,32,512]{2,1,0:T(8,128)(2,1)} %bitcast.9), calls=%async_computation.1 | async-start | bytes 524288 | tf_op jit(solution)/shard_map/all_to_all | solution.py:85
  1339.1 0.3 convolution_bitcast_fusion.4
  1339.5 1.3 convolution_convert_fusion
  1340.7 4.9 all-to-all-done.1
  1345.6 4.4 all-to-all-start.6
  1350.0 0.7 copy.58
  1350.7 5.8 all-to-all-done.6
  1356.5 0.7 copy.59
  (14 shorter events, 0.1 us)
Async XLA Ops:
  8.4 165.3 %all-to-all-start.2 = ((bf16[32,8,1]{0,2,1:T(2,128)(2,1)}), bf16[32,8,1]{0,2,1:T(2,128)(2,1)S(1)}, u32[]{:S(2)}, u32[]{:S(2)}) async-start(bf16[32,8,1]{0,2,1:T(2,128)(2,1)} %copy.43), calls=%async_computation.2 | async-start | bytes 8192 | tf_op jit(solution)/shard_map/all_to_all | solution.py:49
  173.7 128.0 %all-to-all-start.4 = ((bf16[32,8,512]{2,0,1:T(8,128)(2,1)}), bf16[32,8,512]{2,0,1:T(8,128)(2,1)S(1)}, u32[]{:S(2)}, u32[]{:S(2)}) async-start(bf16[32,8,512]{2,0,1:T(8,128)(2,1)} %bitcast.139), calls=%async_computation.4 | async-start | bytes 524288 | tf_op jit(solution)/shard_map/all_to_all | solution.py:47
  301.7 36.9 %all-to-all-start.3 = ((bf16[32,8,512]{2,0,1:T(8,128)(2,1)}), bf16[32,8,512]{2,0,1:T(8,128)(2,1)S(1)}, u32[]{:S(2)}, u32[]{:S(2)}) async-start(bf16[32,8,512]{2,0,1:T(8,128)(2,1)} %bitcast.140), calls=%async_computation.3 | async-start | bytes 524288 | tf_op jit(solution)/shard_map/all_to_all | solution.py:48
  332.0 694.6 %reduce-scatter.2.cloned.1.call-start = ((), (), s32[]{:S(2)}) async-start(), calls=%async_computation.8 | async-start | bytes 3194880 | tf_op jit(solution)/shard_map/reduce_scatter | solution.py:68
  342.2 0.9 copy-start
  342.2 6.0 copy-start.1
  343.9 10.9 all-to-all-start
  348.3 679.3 %copy-start.2 = (f32[1,8,512]{2,1,0:T(8,128)S(1)}, f32[1,8,512]{2,1,0:T(8,128)}, u32[]{:S(2)}) copy-start(f32[1,8,512]{2,1,0:T(8,128)} %param.16) | copy-start | bytes 49156
  348.3 679.3 %copy-start.3 = (f32[1,8,512]{2,1,0:T(8,128)S(1)}, f32[1,8,512]{2,1,0:T(8,128)}, u32[]{:S(2)}) copy-start(f32[1,8,512]{2,1,0:T(8,128)} %param.15) | copy-start | bytes 49156
  348.3 679.3 %copy-start.4 = (f32[1,8,512]{2,1,0:T(8,128)S(1)}, f32[1,8,512]{2,1,0:T(8,128)}, u32[]{:S(2)}) copy-start(f32[1,8,512]{2,1,0:T(8,128)} %param.14) | copy-start | bytes 49156
  354.8 893.0 %all-to-all-start.5 = ((bf16[32,8,512]{2,0,1:T(8,128)(2,1)}), bf16[32,8,512]{2,0,1:T(8,128)(2,1)S(1)}, u32[]{:S(2)}, u32[]{:S(2)}) async-start(bf16[32,8,512]{2,0,1:T(8,128)(2,1)} %bitcast.138), calls=%async_computation.6 | async-start | bytes 524288 | tf_op jit(solution)/shard_map/all_to_all | solution.py:50
  1247.8 97.8 %all-to-all-start.1 = ((bf16[8,32,512]{2,1,0:T(8,128)(2,1)}), bf16[8,32,512]{2,1,0:T(8,128)(2,1)S(1)}, u32[]{:S(2)}, u32[]{:S(2)}) async-start(bf16[8,32,512]{2,1,0:T(8,128)(2,1)} %bitcast.9), calls=%async_computation.1 | async-start | bytes 524288 | tf_op jit(solution)/shard_map/all_to_all | solution.py:85
  1345.6 10.9 all-to-all-start.6
Sparse Core Ops, SparseCore 0:
  342.4 684.1 reduce-scatter.1
where the time goes:
time: 1370 us; the launch traced here: 1360 us
  waiting for transfers between devices  688 us (50%)
  blocking collectives  440 us (32%)
  starting transfers between devices  201 us (15%)
  between operations  14.8 us (1%)
    reduce_scatter x1, waiting for transfers between devices, local(): lax.psum_scatter(gradient_rows(grad_gate_pre, grad_up_pre, hidden_k, keys...  666 us
    all_to_all x1, starting transfers between devices, local(): lax.all_to_all(first_block, 'head', split_axis=0, concat_axis=1, tiled=True)  91.3 us
    all_gather x1, blocking collectives, local(): lax.all_gather(w_down.astype(jnp.bfloat16), 'tok', axis=1, tiled=True)  76.5 us
    all_gather x1, blocking collectives, local(): lax.all_gather(down_new.astype(jnp.bfloat16), 'tok', axis=1, tiled=True)  73.4 us
    all_gather x1, blocking collectives, local(): lax.all_gather(w_up.astype(jnp.bfloat16), 'tok', axis=1, tiled=True)  73.1 us
    all_gather x1, blocking collectives, local(): lax.all_gather(gate_new.astype(jnp.bfloat16), 'tok', axis=1, tiled=True)  72.8 us
    all_gather x1, blocking collectives, local(): lax.all_gather(up_new.astype(jnp.bfloat16), 'tok', axis=1, tiled=True)  72.6 us
    all_gather x1, blocking collectives, local(): lax.all_gather(w_gate.astype(jnp.bfloat16), 'tok', axis=1, tiled=True)  71.9 us
  transfers between devices with their start and end apart: 8, of which 5 were waited for; matrix products, arithmetic and copies ran while one was open for 1% of the time, Pallas kernels for 0%

commit v1 on v0

--- a/solution.py
+++ b/solution.py
@@ -2,6 +2,23 @@
 import jax.numpy as jnp
 from jax import lax
 from jax.sharding import PartitionSpec as P
+
+
+def supply_all_clusters(xin, link_axis):
+    current_arr = lax.axis_size(link_axis)
+    r2 = lax.axis_index(link_axis)
+    val2, block_last = (current_arr, r2)
+    piece_next, b_next = (xin, 1)
+    while b_next < val2:
+        buffer = []
+        for num in tuple(range(val2)):
+            buffer.append((num, num ^ b_next))
+        even = lax.ppermute(piece_next, axis_name=link_axis, perm=buffer)
+        x_now = jnp.concatenate([piece_next, even], axis=1)
+        long_array = jnp.concatenate([even, piece_next], 1)
+        piece_next = jnp.where(block_last & b_next == 0, x_now, long_array)
+        b_next = 2 * b_next
+    return piece_next
 
 
 def apply_piece(query, gate_b, up_b, down_b):
@@ -57,7 +74,7 @@
     query_b = moved[4].reshape(tokens, heads_local, width)
     targets = (-(rates[:, :, None] * values.astype(jnp.float32))).astype(jnp.bfloat16)
     pieces = (
-        lax.all_gather(w_gate.astype(jnp.bfloat16), "tok", axis=1, tiled=True),
+        supply_all_clusters(w_gate.astype(jnp.bfloat16), link_axis="tok"),
         lax.all_gather(w_up.astype(jnp.bfloat16), "tok", axis=1, tiled=True),
         lax.all_gather(w_down.astype(jnp.bfloat16), "tok", axis=1, tiled=True),
     )

time: 1370 us -> 1330 us (0.971)
  blocking collectives: 440 us -> 368 us
  waiting for transfers between devices: 688 us -> 716 us
    all_gather x1 -> x0, blocking collectives: 71.9 us -> none  [local(): lax.all_gather(w_gate.astype(jnp.bfloat16), 'tok', axis=1, tiled=True)]
    all_to_all x1, starting transfers between devices: 55.9 us -> 8.22 us  [local(): lax.all_to_all(key_one, 'head', split_axis=1, concat_axis=0, tiled=True)]
    ppermute x0 -> x6, waiting for transfers between devices: none -> 28.3 us  [supply_all_clusters(): even = lax.ppermute(piece_next, axis_name=link_axis, perm=buffer)]
    all_to_all x1, starting transfers between devices: 30.4 us -> 56.7 us  [local(): lax.all_to_all(value_one, 'head', split_axis=1, concat_axis=0, tiled=True)]
    ppermute x0 -> x6, starting transfers between devices: none -> 22.3 us  [supply_all_clusters(): even = lax.ppermute(piece_next, axis_name=link_axis, perm=buffer)]
  transfers between devices with their start and end apart: 8 -> 14, of which waited for: 5 -> 10; matrix products, arithmetic and copies ran while one was open for 1% -> 1% of each run, Pallas kernels for 0% -> 0%
where the time goes in v1:
time: 1330 us
  waiting for transfers between devices  716 us (54%)
  blocking collectives  368 us (28%)
  starting transfers between devices  209 us (16%)
  between operations  14.9 us (1%)
    reduce_scatter x1, waiting for transfers between devices, local(): lax.psum_scatter(gradient_rows(grad_gate_pre, grad_up_pre, hidden_k, keys...  666 us
    all_to_all x1, starting transfers between devices, local(): lax.all_to_all(first_block, 'head', split_axis=0, concat_axis=1, tiled=True)  91.3 us
    all_gather x1, blocking collectives, local(): lax.all_gather(w_down.astype(jnp.bfloat16), 'tok', axis=1, tiled=True)  77.6 us
    all_gather x1, blocking collectives, local(): lax.all_gather(gate_new.astype(jnp.bfloat16), 'tok', axis=1, tiled=True)  73.1 us
    all_gather x1, blocking collectives, local(): lax.all_gather(up_new.astype(jnp.bfloat16), 'tok', axis=1, tiled=True)  72.8 us
    all_gather x1, blocking collectives, local(): lax.all_gather(down_new.astype(jnp.bfloat16), 'tok', axis=1, tiled=True)  72.7 us
    all_gather x1, blocking collectives, local(): lax.all_gather(w_up.astype(jnp.bfloat16), 'tok', axis=1, tiled=True)  72.2 us
    all_to_all x1, starting transfers between devices, local(): lax.all_to_all(value_one, 'head', split_axis=1, concat_axis=0, tiled=True)  56.7 us
  transfers between devices with their start and end apart: 14, of which 10 were waited for; matrix products, arithmetic and copies ran while one was open for 1% of the time, Pallas kernels for 0%

profile of v1, /device:TPU:1, one launch (start us, length us, event | category | flops | bytes accessed | tf_op | source)
XLA Modules:
  0.0 1330.6 jit_solution(11076202569131269778)
XLA Ops:
  7.2 0.7 convert_element_type.140
  7.9 4.0 collective-permute-start
  11.9 1.3 copy.56
  13.2 8.0 all-to-all-start.2
  21.2 0.7 convert_bitcast_fusion
  21.9 0.7 convert_element_type.143
  22.6 77.6 %all_gather.16 = bf16[1,512,512]{2,1,0:T(8,128)(2,1)S(1)} all-gather(bf16[1,8,512]{2,1,0:T(8,128)(2,1)S(1)} %convert_element_type.143), channel_id=1, replica_groups=mesh['head'=8,'tok'=64] {'tok'}, dimensions={1}, use_global_device_ids=true | all-gather | bytes 532480 | tf_op jit(solution)/shard_map/all_gather | solution.py:79
  100.2 0.7 convert_element_type.141
  100.9 72.2 %all_gather.15 = bf16[1,512,512]{2,1,0:T(8,128)(2,1)S(1)} all-gather(bf16[1,8,512]{2,1,0:T(8,128)(2,1)S(1)} %convert_element_type.141), channel_id=1, replica_groups=mesh['head'=8,'tok'=64] {'tok'}, dimensions={1}, use_global_device_ids=true | all-gather | bytes 532480 | tf_op jit(solution)/shard_map/all_gather | solution.py:78
  173.1 1.7 copy.82
  174.8 1.7 copy.81
  176.5 56.7 %all-to-all-start.3 = ((bf16[32,8,512]{2,0,1:T(8,128)(2,1)}), bf16[32,8,512]{2,0,1:T(8,128)(2,1)S(1)}, u32[]{:S(2)}, u32[]{:S(2)}) async-start(bf16[32,8,512]{2,0,1:T(8,128)(2,1)} %bitcast.151), calls=%async_computation.3 | async-start | bytes 524288 | tf_op jit(solution)/shard_map/all_to_all | solution.py:65
  233.3 3.3 collective-permute-start.1
  236.6 2.7 collective-permute-done.1
  239.3 1.9 collective-permute-start.2
  241.2 2.7 collective-permute-done.2
  244.0 1.9 collective-permute-start.3
  245.9 4.4 collective-permute-done.3
  250.3 2.8 collective-permute-start.4
  253.2 8.2 all-to-all-start.4
  261.5 0.4 fusion.9
  261.9 6.3 all-to-all-done.4
  268.6 0.7 collective-permute-done.4
  269.4 8.4 collective-permute-start.5
  277.9 17.8 %collective-permute-done.5 = bf16[1,256,512]{2,1,0:T(8,128)(2,1)S(1)} collective-permute-done((bf16[1,256,512]{2,1,0:T(8,128)(2,1)S(1)}, bf16[1,256,512]{2,1,0:T(8,128)(2,1)S(1)}, u32[]{:S(2)}, u32[]{:S(2)}) %collective-permute-start.5) | collective-permute-done | bytes 262176 | tf_op jit(solution)/shard_map/ppermute | solution.py:16
  295.7 0.4 convolution_bitcast_fusion.5
  296.4 0.4 convolution_bitcast_fusion.2
  297.2 2.0 pad_maximum_fusion
  299.1 0.9 copy-done
  300.1 0.7 copy.83
  300.8 14.2 %all-to-all-start = ((bf16[32,8,512]{2,0,1:T(8,128)(2,1)}), bf16[32,8,512]{2,0,1:T(8,128)(2,1)S(1)}, u32[]{:S(2)}, u32[]{:S(2)}) async-start(bf16[32,8,512]{2,0,1:T(8,128)(2,1)} %bitcast.152), calls=%async_computation | async-start | bytes 524288 | tf_op jit(solution)/shard_map/all_to_all | solution.py:63
  315.0 0.7 copy.80
  316.4 5.1 all-to-all-done
  321.5 4.4 all-to-all-start.5
  326.2 1.5 convolution_convert_fusion.1
  327.8 665.5 %reduce-scatter.2.cloned.1.call-done = f32[8,1,3,512]{3,0,2,1:T(8,128)} async-done(((f32[512,1,3,512]{3,0,2,1:T(8,128)}), f32[8,1,3,512]{3,0,2,1:T(8,128)}) %reduce-scatter.2.cloned.1.call-update) | async-done | bytes 49168 | tf_op jit(solution)/shard_map/reduce_scatter | solution.py:85
  993.3 0.9 multiply_reduce_fusion.1
  994.2 1.5 fusion.45
  995.7 72.8 %all_gather.19 = bf16[1,512,512]{2,1,0:T(8,128)(2,1)S(1)} all-gather(bf16[1,8,512]{2,1,0:T(8,128)(2,1)S(1)} %get-tuple-element.14), channel_id=1, replica_groups=mesh['head'=8,'tok'=64] {'tok'}, dimensions={1}, use_global_device_ids=true | all-gather | bytes 532480 | tf_op jit(solution)/shard_map/all_gather | solution.py:96
  1068.5 72.7 %all_gather.17 = bf16[1,512,512]{2,1,0:T(8,128)(2,1)S(1)} all-gather(bf16[1,8,512]{2,1,0:T(8,128)(2,1)S(1)} %get-tuple-element.16), channel_id=1, replica_groups=mesh['head'=8,'tok'=64] {'tok'}, dimensions={1}, use_global_device_ids=true | all-gather | bytes 532480 | tf_op jit(solution)/shard_map/all_gather | solution.py:97
  1141.2 73.1 %all_gather.18 = bf16[1,512,512]{2,1,0:T(8,128)(2,1)S(1)} all-gather(bf16[1,8,512]{2,1,0:T(8,128)(2,1)S(1)} %get-tuple-element.8), channel_id=1, replica_groups=mesh['head'=8,'tok'=64] {'tok'}, dimensions={1}, use_global_device_ids=true | all-gather | bytes 532480 | tf_op jit(solution)/shard_map/all_gather | solution.py:95
  1214.3 91.3 %all-to-all-start.1 = ((bf16[8,32,512]{2,1,0:T(8,128)(2,1)}), bf16[8,32,512]{2,1,0:T(8,128)(2,1)S(1)}, u32[]{:S(2)}, u32[]{:S(2)}) async-start(bf16[8,32,512]{2,1,0:T(8,128)(2,1)} %bitcast.20), calls=%async_computation.1 | async-start | bytes 524288 | tf_op jit(solution)/shard_map/all_to_all | solution.py:102
  1305.9 1.5 convolution_convert_fusion
  1307.5 4.7 all-to-all-done.1
  1312.1 4.4 all-to-all-start.6
  1316.5 0.7 copy.74
  1317.2 5.8 all-to-all-done.6
  1323.0 0.7 copy.75
  (36 shorter events, 2.2 us)
Async XLA Ops:
  7.9 225.4 %collective-permute-start = (bf16[1,8,512]{2,1,0:T(8,128)(2,1)S(1)}, bf16[1,8,512]{2,1,0:T(8,128)(2,1)S(1)}, u32[]{:S(2)}, u32[]{:S(2)}) collective-permute-start(bf16[1,8,512]{2,1,0:T(8,128)(2,1)S(1)} %convert_element_type.140), channel_id=1, source_target_pairs={{0,1},{1,0},{2,3},{3,2},{4,5},{5,4},{6,7},{7,6},{8,9},{9,8},{10,11... | collective-permute-start | bytes 24584 | tf_op jit(solution)/shard_map/ppermute | solution.py:16
  13.2 163.3 %all-to-all-start.2 = ((bf16[32,8,1]{0,2,1:T(2,128)(2,1)}), bf16[32,8,1]{0,2,1:T(2,128)(2,1)S(1)}, u32[]{:S(2)}, u32[]{:S(2)}) async-start(bf16[32,8,1]{0,2,1:T(2,128)(2,1)} %copy.56), calls=%async_computation.2 | async-start | bytes 8192 | tf_op jit(solution)/shard_map/all_to_all | solution.py:66
  176.5 76.7 %all-to-all-start.3 = ((bf16[32,8,512]{2,0,1:T(8,128)(2,1)}), bf16[32,8,512]{2,0,1:T(8,128)(2,1)S(1)}, u32[]{:S(2)}, u32[]{:S(2)}) async-start(bf16[32,8,512]{2,0,1:T(8,128)(2,1)} %bitcast.151), calls=%async_computation.3 | async-start | bytes 524288 | tf_op jit(solution)/shard_map/all_to_all | solution.py:65
  233.3 6.0 collective-permute-start.1
  239.3 4.7 collective-permute-start.2
  244.0 6.3 collective-permute-start.3
  250.3 19.0 %collective-permute-start.4 = (bf16[1,128,512]{2,1,0:T(8,128)(2,1)S(1)}, bf16[1,128,512]{2,1,0:T(8,128)(2,1)S(1)}, u32[]{:S(2)}, u32[]{:S(2)}) collective-permute-start(bf16[1,128,512]{2,1,0:T(8,128)(2,1)S(1)} %maximum_select_fusion.4), channel_id=1, source_target_pairs={{0,16},{1,17},{2,18},{3,19},{4,20},{5,21},{6,22},{7,23},{8,24},{9,... | collective-permute-start | bytes 393224 | tf_op jit(solution)/shard_map/ppermute | solution.py:16
  253.2 15.0 %all-to-all-start.4 = ((bf16[32,8,512]{2,0,1:T(8,128)(2,1)}), bf16[32,8,512]{2,0,1:T(8,128)(2,1)S(1)}, u32[]{:S(2)}, u32[]{:S(2)}) async-start(bf16[32,8,512]{2,0,1:T(8,128)(2,1)} %bitcast.150), calls=%async_computation.4 | async-start | bytes 524288 | tf_op jit(solution)/shard_map/all_to_all | solution.py:64
  261.5 731.8 %reduce-scatter.2.cloned.1.call-start = ((), (), s32[]{:S(2)}) async-start(), calls=%async_computation.8 | async-start | bytes 3194880 | tf_op jit(solution)/shard_map/reduce_scatter | solution.py:85
  269.4 26.3 %collective-permute-start.5 = (bf16[1,256,512]{2,1,0:T(8,128)(2,1)S(1)}, bf16[1,256,512]{2,1,0:T(8,128)(2,1)S(1)}, u32[]{:S(2)}, u32[]{:S(2)}) collective-permute-start(bf16[1,256,512]{2,1,0:T(8,128)(2,1)S(1)} %maximum_select_fusion.2), channel_id=1, source_target_pairs={{0,32},{1,33},{2,34},{3,35},{4,36},{5,37},{6,38},{7,39},{8,40},{9,... | collective-permute-start | bytes 786440 | tf_op jit(solution)/shard_map/ppermute | solution.py:16
  299.1 0.9 copy-start
  299.1 15.9 %copy-start.1 = (bf16[32,4096]{1,0:T(8,128)(2,1)S(1)}, bf16[32,4096]{1,0:T(8,128)(2,1)}, u32[]{:S(2)}) copy-start(bf16[32,4096]{1,0:T(8,128)(2,1)} %param.13) | copy-start | bytes 786436
  300.8 20.7 %all-to-all-start = ((bf16[32,8,512]{2,0,1:T(8,128)(2,1)}), bf16[32,8,512]{2,0,1:T(8,128)(2,1)S(1)}, u32[]{:S(2)}, u32[]{:S(2)}) async-start(bf16[32,8,512]{2,0,1:T(8,128)(2,1)} %bitcast.152), calls=%async_computation | async-start | bytes 524288 | tf_op jit(solution)/shard_map/all_to_all | solution.py:63
  321.5 892.8 %all-to-all-start.5 = ((bf16[32,8,512]{2,0,1:T(8,128)(2,1)}), bf16[32,8,512]{2,0,1:T(8,128)(2,1)S(1)}, u32[]{:S(2)}, u32[]{:S(2)}) async-start(bf16[32,8,512]{2,0,1:T(8,128)(2,1)} %bitcast.149), calls=%async_computation.6 | async-start | bytes 524288 | tf_op jit(solution)/shard_map/all_to_all | solution.py:67
  325.9 668.3 %copy-start.2 = (f32[1,8,512]{2,1,0:T(8,128)S(1)}, f32[1,8,512]{2,1,0:T(8,128)}, u32[]{:S(2)}) copy-start(f32[1,8,512]{2,1,0:T(8,128)} %param.14) | copy-start | bytes 49156
  325.9 668.3 %copy-start.3 = (f32[1,8,512]{2,1,0:T(8,128)S(1)}, f32[1,8,512]{2,1,0:T(8,128)}, u32[]{:S(2)}) copy-start(f32[1,8,512]{2,1,0:T(8,128)} %param.16) | copy-start | bytes 49156
  325.9 668.4 %copy-start.4 = (f32[1,8,512]{2,1,0:T(8,128)S(1)}, f32[1,8,512]{2,1,0:T(8,128)}, u32[]{:S(2)}) copy-start(f32[1,8,512]{2,1,0:T(8,128)} %param.15) | copy-start | bytes 49156
  1214.3 97.8 %all-to-all-start.1 = ((bf16[8,32,512]{2,1,0:T(8,128)(2,1)}), bf16[8,32,512]{2,1,0:T(8,128)(2,1)S(1)}, u32[]{:S(2)}, u32[]{:S(2)}) async-start(bf16[8,32,512]{2,1,0:T(8,128)(2,1)} %bitcast.20), calls=%async_computation.1 | async-start | bytes 524288 | tf_op jit(solution)/shard_map/all_to_all | solution.py:102
  1312.1 10.9 all-to-all-start.6
Sparse Core Ops, SparseCore 0:
  299.3 693.9 reduce-scatter.1
